TPU v7x, 128 devices: a whole 4x4x4 slice. The times are simulated.
128 devices in a mesh: gx: 4 (over y_hi, core), gy: 4 (over z), ta: 8 (over x, y_lo).
Axes of the slice: x: 4, y: 4 (y_hi: 2, y_lo: 2; y = y_hi * 2 + y_lo), z: 4, core: 2. Of those that a mesh axis runs over, the one named last changes fastest.
Arguments:
- features: bfloat16 [32, 16, 16, 128, 256], P('ta', 'gx', 'gy'), may hold values from -6 to 6
- neighbours: int32 [16, 16, 4], P('gx', 'gy'), may hold values from 0 to 8, as said below
- adjacency: int32 [16, 16, 4, 128, 128], P('gx', 'gy'), may hold values 0 or 1
- w_space: bfloat16 [256, 256], replicated, may hold values from -0.375 to 0.375
- w_time: bfloat16 [3, 256, 256], replicated, may hold values from -0.21875 to 0.21875
- cotangent: bfloat16 [32, 16, 16, 128, 256], P('ta', 'gx', 'gy'), may hold values from -6 to 6
Outputs:
- updated: bfloat16 [32, 16, 16, 128, 256], P('ta', 'gx', 'gy')
- grad_space: float32 [256, 256], replicated
- grad_time: float32 [3, 256, 256], replicated
Inputs may be any that keep to these rules, and one draw needn't show every extreme that they name: `neighbours`: the 4 codes of a tile are distinct; code c names the tile c // 3 - 1 tiles away along x and c % 3 - 1 tiles away along y, periodically.
All inputs are finite; a program needn't handle non-finite values. No bound on the sum of `adjacency` on one device may be relied on, other than what follows from the above.
Results may differ from a plain program's by a relative error of at most 0.0068.
Values may be sent and summed in bfloat16 or wider, within the bound.
No kernel may reach another device: no remote copies, remote signals or barrier semaphores. Data moves between devices by JAX's collectives and lax.ppermute only.
A program may use at most 128 MiB of HBM per device.

v0:
```python
import math
import jax
import jax.numpy as jnp
from jax import lax
from jax.sharding import PartitionSpec as P


def with_halo(block, sides, width):
    for axis, dim in sides:
        count = lax.axis_size(axis)
        forward = [(i, i + 1) for i in range(count - 1)]
        forward.append((count - 1, 0))
        backward = [(target, source) for source, target in forward]
        low = lax.ppermute(
            lax.slice_in_dim(block, block.shape[dim] - width, None, axis=dim), axis, forward
        )
        high = lax.ppermute(lax.slice_in_dim(block, 0, width, axis=dim), axis, backward)
        block = jnp.concatenate([low, block, high], axis=dim)
    return block


def from_behind(block, axis, distance):
    devices = range(lax.axis_size(axis))
    route = [(i - distance, i) for i in devices if i - distance in devices]
    return lax.ppermute(block, axis, route)


def shards(features, neighbours, adjacency, w_space, w_time, cotangent):
    frames, tiles_x, tiles_y, lipids, feat_width = features.shape
    tap_count = w_time.shape[0]
    slot_count = neighbours.shape[2]
    behind = tap_count - 1
    tile_count = tiles_x * tiles_y
    row_count = tile_count * lipids
    extended = with_halo(features, (("gx", 1), ("gy", 2)), 1)
    flat_tiles = extended.reshape(frames, (tiles_x + 2) * (tiles_y + 2), lipids, feat_width)
    along_x = jnp.arange(tiles_x, dtype=jnp.int32)[:, None]
    along_y = jnp.arange(tiles_y, dtype=jnp.int32)[None, :]
    summed = jnp.zeros((frames, tile_count, lipids, feat_width), jnp.float32)
    for slot_pos in range(slot_count):
        offset_code = neighbours[:, :, slot_pos]
        source_index = (
            (along_x + offset_code // 3) * (tiles_y + 2) + along_y + offset_code % 3
        ).reshape(-1)
        picked = jnp.take(flat_tiles, source_index, axis=1)
        lipid_mask = (
            adjacency[:, :, slot_pos].reshape(tile_count, lipids, lipids).astype(jnp.bfloat16)
        )
        summed = summed + jnp.einsum(
            "tij,ftjc->ftic", lipid_mask, picked, preferred_element_type=jnp.float32
        )
    aggregate = (0.18 * summed).astype(jnp.bfloat16).reshape(frames * row_count, feat_width)
    projected = jnp.dot(aggregate, w_space, preferred_element_type=jnp.float32).astype(jnp.bfloat16)
    projected = projected.reshape(frames, row_count, feat_width)
    mixed = jnp.zeros((frames, row_count, feat_width), jnp.float32)
    blank = jnp.zeros((behind, row_count, feat_width), jnp.bfloat16)
    padded = jnp.concatenate([blank, projected, blank], axis=0)
    for offset in range(tap_count):
        window = padded[behind - offset : behind - offset + frames].reshape(-1, feat_width)
        mixed = mixed + jnp.dot(window, w_time[offset], preferred_element_type=jnp.float32).reshape(
            frames, row_count, feat_width
        )
    partial_terms = jnp.zeros((behind, row_count, feat_width), jnp.float32)
    for offset in range(1, tap_count):
        window = padded[behind + frames - offset : behind + frames - offset + behind].reshape(
            -1, feat_width
        )
        partial_terms = partial_terms + jnp.dot(
            window, w_time[offset], preferred_element_type=jnp.float32
        ).reshape(behind, row_count, feat_width)
    carried = from_behind(partial_terms, "ta", 1)
    mixed = mixed + jnp.concatenate(
        [carried, jnp.zeros((frames - behind, row_count, feat_width), jnp.float32)], axis=0
    )
    sigmoid_z = jax.nn.sigmoid(mixed)
    own = features.reshape(frames, row_count, feat_width).astype(jnp.float32)
    updated = (own + mixed * sigmoid_z).astype(jnp.bfloat16).reshape(features.shape)
    grad_in = cotangent.reshape(frames, row_count, feat_width).astype(jnp.float32)
    grad_mixed = (grad_in * sigmoid_z * (1.0 + mixed * (1.0 - sigmoid_z))).astype(jnp.bfloat16)
    next_grads = from_behind(grad_mixed[:behind], "ta", -1)
    joined = jnp.concatenate([grad_mixed, next_grads], axis=0)
    proj_rows = projected.reshape(-1, feat_width)
    contract = (((0,), (0,)), ((), ()))
    row_scale = 1.0 / math.sqrt(
        frames * row_count * lax.axis_size("gx") * lax.axis_size("gy") * lax.axis_size("ta")
    )
    parts = []
    for offset in range(tap_count):
        later = joined[offset : offset + frames].reshape(-1, feat_width)
        parts.append(
            lax.dot_general(proj_rows, later, contract, preferred_element_type=jnp.float32)
        )
    grad_proj = jnp.zeros((frames * row_count, feat_width), jnp.float32)
    for offset in range(tap_count):
        later = joined[offset : offset + frames].reshape(-1, feat_width)
        grad_proj = grad_proj + jnp.dot(later, w_time[offset].T, preferred_element_type=jnp.float32)
    grad_proj = grad_proj.astype(jnp.bfloat16)
    grad_space, grad_time = lax.psum(
        (
            lax.dot_general(aggregate, grad_proj, contract, preferred_element_type=jnp.float32),
            jnp.stack(parts),
        ),
        ("gx", "gy", "ta"),
    )
    return (updated, grad_space * row_scale, grad_time * row_scale)


def solution(mesh):
    in_specs = (
        P("ta", "gx", "gy", None, None),
        P("gx", "gy", None),
        P("gx", "gy", None, None, None),
        P(),
        P(),
        P("ta", "gx", "gy", None, None),
    )
    out_specs = (P("ta", "gx", "gy", None, None), P(), P())
    return jax.shard_map(shards, mesh=mesh, in_specs=in_specs, out_specs=out_specs, check_vma=False)
```

profile of v0, /device:TPU:1, one launch (start us, length us, event | category | flops | bytes accessed | tf_op | source)
XLA Modules:
  0.0 478.1 jit_solution(4176581645567628972)
XLA Ops:
  7.2 1.8 fusion.64
  9.1 4.4 collective-permute-start
  13.5 22.5 %collective-permute-done = bf16[4,1,4,128,256]{4,3,2,1,0:T(8,128)(2,1)S(1)} collective-permute-done((bf16[4,1,4,128,256]{4,3,2,1,0:T(8,128)(2,1)S(1)}, bf16[4,1,4,128,256]{4,3,2,1,0:T(8,128)(2,1)S(1)}, u32[]{:S(2)}, u32[]{:S(2)}) %collective-permute-start) | collective-permute-done | bytes 1048608 | tf_op jit(solution)/shard_map/ppermute | solution.py:14
  36.1 0.5 constant_dynamic-update-slice_fusion.1
  36.6 0.3 collective-permute-done.1
  36.9 2.7 copy-done.4
  39.6 1.9 fusion.63
  41.5 1.7 collective-permute-start.2
  43.2 2.1 collective-permute-start.3
  45.5 0.4 fusion.54
  46.3 0.7 divide_reduce_fusion
  47.7 2.8 convert.11
  50.6 1.1 fusion.65
  51.7 28.7 %collective-permute-done.2 = bf16[4,6,1,128,256]{4,3,2,1,0:T(8,128)(2,1)S(1)} collective-permute-done((bf16[4,6,1,128,256]{4,3,2,1,0:T(8,128)(2,1)}, bf16[4,6,1,128,256]{4,3,2,1,0:T(8,128)(2,1)S(1)}, u32[]{:S(2)}, u32[]{:S(2)}) %collective-permute-start.2) | collective-permute-done | bytes 1572896 | tf_op jit(solution)/shard_map/ppermute | solution.py:14
  80.4 5.7 %pad_maximum_fusion = bf16[4,6,6,128,256]{4,3,2,1,0:T(8,128)(2,1)} fusion(bf16[4,6,1,128,256]{4,3,2,1,0:T(8,128)(2,1)} %collective-permute-done.3, bf16[4,6,4,128,256]{4,3,2,1,0:T(8,128)(2,1)S(1)} %copy-done.5, bf16[4,6,1,128,256]{4,3,2,1,0:T(8,128)(2,1)S(1)} %collective-permute-done.2), kind=kLoop, calls=%fused_computation.8 | loop fusion | flops 9437184 | bytes 18874368 | tf_op jit(solution)/shard_map/concatenate | solution.py:18
  86.1 6.4 %gather_fusion.3 = bf16[16,4,128,256]{3,2,1,0:T(8,128)(2,1)} fusion(bf16[4,36,128,256]{3,2,1,0:T(8,128)(2,1)} %bitcast.110, s32[1024]{0:T(1024)S(1)} %get-tuple-element.44), kind=kCustom, calls=%fused_computation.3.clone | custom fusion | bytes 8388672 | tf_op jit(solution)/shard_map/jit(_take)/gather | solution.py:45
  92.5 6.5 %gather_fusion.2 = bf16[16,4,128,256]{3,2,1,0:T(8,128)(2,1)} fusion(bf16[4,36,128,256]{3,2,1,0:T(8,128)(2,1)} %bitcast.111, s32[1024]{0:T(1024)S(1)} %get-tuple-element.45), kind=kCustom, calls=%fused_computation.2.clone | custom fusion | bytes 8388672 | tf_op jit(solution)/shard_map/jit(_take)/gather | solution.py:45
  99.0 6.6 %gather_fusion.1 = bf16[16,4,128,256]{3,2,1,0:T(8,128)(2,1)} fusion(bf16[4,36,128,256]{3,2,1,0:T(8,128)(2,1)} %bitcast.112, s32[1024]{0:T(1024)S(1)} %get-tuple-element.46), kind=kCustom, calls=%fused_computation.1.clone | custom fusion | bytes 8388672 | tf_op jit(solution)/shard_map/jit(_take)/gather | solution.py:45
  105.6 6.5 %gather_fusion = bf16[16,4,128,256]{3,2,1,0:T(8,128)(2,1)} fusion(bf16[4,36,128,256]{3,2,1,0:T(8,128)(2,1)} %bitcast.113, s32[1024]{0:T(1024)S(1)} %get-tuple-element.47), kind=kCustom, calls=%fused_computation.clone | custom fusion | bytes 8388672 | tf_op jit(solution)/shard_map/jit(_take)/gather | solution.py:45
  112.1 3.8 fusion.8
  115.9 4.5 fusion.12
  120.5 4.5 fusion.10
  125.0 10.2 %fusion.5 = bf16[4,16,128,256]{3,2,0,1:T(8,128)(2,1)} fusion(f32[16,4,256,128]{2,3,1,0:T(8,128)S(1)} %fusion.8, f32[16,4,256,128]{2,3,1,0:T(8,128)} %fusion.12, f32[16,4,256,128]{2,3,1,0:T(8,128)} %fusion.10, bf16[16,128,128,1]{2,1,3,0:T(8,128)(2,1)S(1)} %bitcast.119, bf16[16,4,128,256]{3,2,1,0:T(8,128)(2,1)} %gather_fusion.3, ...), kind=kOutput, calls=%fused_computation.20 | convolution fusion | flops 549453824 | bytes 34078736 | tf_op jit(solution)/shard_map/tij,ftjc->ftic/dot_general | solution.py:49
  135.2 2.5 copy.9
  137.7 1.2 convolution_convert_fusion
  138.9 0.6 copy-done.3
  139.7 0.9 copy-done.9
  140.6 0.7 fusion.29
  141.3 0.7 convolution_add_fusion.2
  142.0 4.1 collective-permute-start.4
  146.2 4.5 fusion.35
  150.6 4.5 fusion.38
  155.1 78.7 %collective-permute-done.4 = f32[2,2048,256]{2,1,0:T(8,128)} collective-permute-done((f32[2,2048,256]{2,1,0:T(8,128)S(1)}, f32[2,2048,256]{2,1,0:T(8,128)}, u32[]{:S(2)}, u32[]{:S(2)}) %collective-permute-start.4) | collective-permute-done | bytes 4194336 | tf_op jit(solution)/shard_map/ppermute | solution.py:25
  233.8 14.0 %fusion.2 = (bf16[4,2048,256]{2,1,0:T(8,128)(2,1)S(1)}, bf16[4,2048,256]{2,1,0:T(8,128)(2,1)}) fusion(bf16[4,4,4,128,256]{4,3,2,1,0:T(8,128)(2,1)} %param.13, bf16[4,4,4,128,256]{4,3,2,1,0:T(8,128)(2,1)} %param.8, f32[2,2048,256]{2,1,0:T(8,128)} %collective-permute-done.4, bf16[4,2048,256]{2,1,0:T(8,128)(2,1)S(1)} %bitcast.105, ...), kind=kOutput, calls=%fused_computation.11 | convolution fusion | flops 572522496 | bytes 42074112 | tf_op jit(solution)/shard_map/dot_general | solution.py:60
  247.9 1.3 collective-permute-start.5
  249.2 1.3 fusion.40
  250.5 1.3 convolution_bitcast_fusion.2
  251.8 45.1 %collective-permute-done.5 = bf16[2,2048,256]{2,1,0:T(8,128)(2,1)S(1)} collective-permute-done((bf16[2,2048,256]{2,1,0:T(8,128)(2,1)S(1)}, bf16[2,2048,256]{2,1,0:T(8,128)(2,1)S(1)}, u32[]{:S(2)}, u32[]{:S(2)}) %collective-permute-start.5) | collective-permute-done | bytes 2097184 | tf_op jit(solution)/shard_map/ppermute | solution.py:25
  296.9 0.8 pad_maximum_fusion.1
  297.8 1.3 convolution_bitcast_fusion.1
  299.1 0.7 copy-done.2
  299.8 1.3 convolution_bitcast_fusion
  301.1 4.5 convolution_add_fusion.1
  305.6 9.1 %fusion.28 = f32[256,256]{1,0:T(8,128)} fusion(bf16[8192,256]{1,0:T(8,128)(2,1)} %bitcast.117, f32[8192,256]{1,0:T(8,128)} %convolution_add_fusion.1, bf16[8192,256]{1,0:T(8,128)(2,1)} %bitcast.115, bf16[3,256,256]{2,1,0:T(8,128)(2,1)S(1)} %copy-done.9), kind=kOutput, calls=%fused_computation.47 | convolution fusion | flops 2151677952 | bytes 17170432 | tf_op jit(solution)/shard_map/dot_general | solution.py:100
  314.7 0.9 pad_maximum_fusion.2
  315.7 151.8 %all-reduce.6.cloned.1.call-done = (f32[256,256]{1,0:T(8,128)}, f32[3,256,256]{2,1,0:T(8,128)}) async-done(((f32[256,256]{1,0:T(8,128)}, f32[3,256,256]{2,1,0:T(8,128)}), (f32[256,256]{1,0:T(8,128)}, f32[3,256,256]{2,1,0:T(8,128)})) %all-reduce.6.cloned.1.call-update) | async-done | bytes 1048592 | tf_op jit(solution)/shard_map/psum | solution.py:98
  467.5 1.7 broadcast_multiply_fusion.1
  469.1 2.1 broadcast_multiply_fusion
  (47 shorter events, 1.8 us)
Async XLA Ops:
  7.2 130.5 %copy-start = (bf16[256,256]{1,0:T(8,128)(2,1)S(1)}, bf16[256,256]{1,0:T(8,128)(2,1)}, u32[]{:S(2)}) copy-start(bf16[256,256]{1,0:T(8,128)(2,1)} %param.11) | copy-start | bytes 393220
  7.2 460.3 %all-reduce.6.cloned.1.call-start = ((), (), s32[]{:S(2)}) async-start(), calls=%async_computation | async-start | bytes 2097152 | tf_op jit(solution)/shard_map/psum | solution.py:98
  7.2 28.8 %copy-start.8 = (bf16[4,4,4,128,256]{4,3,2,1,0:T(8,128)(2,1)S(1)}, bf16[4,4,4,128,256]{4,3,2,1,0:T(8,128)(2,1)}, u32[]{:S(2)}) copy-start(bf16[4,4,4,128,256]{4,3,2,1,0:T(8,128)(2,1)} %param.8) | copy-start | bytes 12582916
  9.1 26.9 %collective-permute-start = (bf16[4,1,4,128,256]{4,3,2,1,0:T(8,128)(2,1)S(1)}, bf16[4,1,4,128,256]{4,3,2,1,0:T(8,128)(2,1)S(1)}, u32[]{:S(2)}, u32[]{:S(2)}) collective-permute-start(bf16[4,1,4,128,256]{4,3,2,1,0:T(8,128)(2,1)S(1)} %get-tuple-element.33), channel_id=1, source_target_pairs={{0,32},{32,64},{64,96},{96,0},{1,33},{33,65},{65,97},{97,1},{2,34}... | collective-permute-start | bytes 3145736 | tf_op jit(solution)/shard_map/ppermute | solution.py:14
  13.5 23.4 %collective-permute-start.1 = (bf16[4,1,4,128,256]{4,3,2,1,0:T(8,128)(2,1)S(1)}, bf16[4,1,4,128,256]{4,3,2,1,0:T(8,128)(2,1)S(1)}, u32[]{:S(2)}, u32[]{:S(2)}) collective-permute-start(bf16[4,1,4,128,256]{4,3,2,1,0:T(8,128)(2,1)S(1)} %get-tuple-element.32), channel_id=1, source_target_pairs={{32,0},{64,32},{96,64},{0,96},{33,1},{65,33},{97,65},{1,97},{34,2}... | collective-permute-start | bytes 3145736 | tf_op jit(solution)/shard_map/ppermute | solution.py:17
  36.6 8.9 %copy-start.11 = (s32[4,4,4]{2,1,0:T(4,128)S(1)}, s32[4,4,4]{2,1,0:T(4,128)}, u32[]{:S(2)}) copy-start(s32[4,4,4]{2,1,0:T(4,128)} %param.9) | copy-start | bytes 772
  36.9 2.7 copy-start.4
  41.5 38.9 %collective-permute-start.2 = (bf16[4,6,1,128,256]{4,3,2,1,0:T(8,128)(2,1)}, bf16[4,6,1,128,256]{4,3,2,1,0:T(8,128)(2,1)S(1)}, u32[]{:S(2)}, u32[]{:S(2)}) collective-permute-start(bf16[4,6,1,128,256]{4,3,2,1,0:T(8,128)(2,1)} %get-tuple-element.30), channel_id=1, source_target_pairs={{0,8},{8,16},{16,24},{24,0},{1,9},{9,17},{17,25},{25,1},{2,10},{10... | collective-permute-start | bytes 4718600 | tf_op jit(solution)/shard_map/ppermute | solution.py:14
  43.2 37.2 %collective-permute-start.3 = (bf16[4,6,1,128,256]{4,3,2,1,0:T(8,128)(2,1)}, bf16[4,6,1,128,256]{4,3,2,1,0:T(8,128)(2,1)}, u32[]{:S(2)}, u32[]{:S(2)}) collective-permute-start(bf16[4,6,1,128,256]{4,3,2,1,0:T(8,128)(2,1)} %get-tuple-element.31), channel_id=1, source_target_pairs={{8,0},{16,8},{24,16},{0,24},{9,1},{17,9},{25,17},{1,25},{10,2},{18... | collective-permute-start | bytes 4718600 | tf_op jit(solution)/shard_map/ppermute | solution.py:17
  47.6 32.7 %copy-start.5 = (bf16[4,6,4,128,256]{4,3,2,1,0:T(8,128)(2,1)S(1)}, bf16[4,6,4,128,256]{4,3,2,1,0:T(8,128)(2,1)}, u32[]{:S(2)}) copy-start(bf16[4,6,4,128,256]{4,3,2,1,0:T(8,128)(2,1)} %copy-done.4) | copy-start | bytes 18874372
  112.1 3.8 copy-start.7
  112.1 3.8 copy-start.10
  115.9 4.6 copy-start.6
  137.7 1.9 copy-start.3
  139.6 1.0 copy-start.9
  142.0 91.8 %collective-permute-start.4 = (f32[2,2048,256]{2,1,0:T(8,128)S(1)}, f32[2,2048,256]{2,1,0:T(8,128)}, u32[]{:S(2)}, u32[]{:S(2)}) collective-permute-start(f32[2,2048,256]{2,1,0:T(8,128)S(1)} %convolution_add_fusion.2), channel_id=1, source_target_pairs={{0,1},{1,2},{2,3},{3,4},{4,5},{5,6},{6,7},{8,9},{9,10},{10,11},{11... | collective-permute-start | bytes 12582920 | tf_op jit(solution)/shard_map/ppermute | solution.py:25
  247.9 49.0 %collective-permute-start.5 = (bf16[2,2048,256]{2,1,0:T(8,128)(2,1)S(1)}, bf16[2,2048,256]{2,1,0:T(8,128)(2,1)S(1)}, u32[]{:S(2)}, u32[]{:S(2)}) collective-permute-start(bf16[2,2048,256]{2,1,0:T(8,128)(2,1)S(1)} %slice.118), channel_id=1, source_target_pairs={{1,0},{2,1},{3,2},{4,3},{5,4},{6,5},{7,6},{9,8},{10,9},{11,10},{12... | collective-permute-start | bytes 6291464 | tf_op jit(solution)/shard_map/ppermute | solution.py:25
  297.8 2.0 copy-start.2
  305.6 165.6 %copy-start.1 = (bf16[256,256]{1,0:T(8,128)(2,1)S(1)}, bf16[256,256]{1,0:T(8,128)(2,1)}, u32[]{:S(2)}) copy-start(bf16[256,256]{1,0:T(8,128)(2,1)} %param.11) | copy-start | bytes 393220
Sparse Core Ops, SparseCore 0:
  315.8 151.6 all-reduce.5
where the time goes:
time: 479 us; the launch traced here: 478 us
  waiting for transfers between devices  327 us (68%)
  matrix products  67.5 us (14%)
  local copies, waits for them, and re-layouts  40.2 us (8%)
  other arithmetic  15.3 us (3%)
  between operations  14.3 us (3%)
  starting transfers between devices  13.7 us (3%)
    psum x1, waiting for transfers between devices, shards(): lax.psum((lax.dot_general(aggregate, grad_proj, contract, preferred_eleme...  152 us
    ppermute x2, waiting for transfers between devices, from_behind(): return lax.ppermute(block, axis, route)  124 us
    ppermute x2, waiting for transfers between devices, with_halo(): lax.ppermute(lax.slice_in_dim(block, block.shape[dim] - width, None, axis...  51.2 us
    gather x4, local copies, waits for them, and re-layouts, shards(): picked = jnp.take(flat_tiles, source_index, axis=1)  25.9 us
    dot_general x5, matrix products, shards(): jnp.dot(window, w_time[offset], preferred_element_type=jnp.float32)  24.4 us
    dot_general x4, matrix products, shards(): jnp.einsum('tij,ftjc->ftic', lipid_mask, picked, preferred_element_type=j...  23.1 us
  transfers between devices with their start and end apart: 7, of which 6 were waited for; matrix products, arithmetic and copies ran while one was open for 4% of the time, Pallas kernels for 0%

commit v1 on v0

--- a/solution.py
+++ b/solution.py
@@ -96,11 +96,14 @@
         grad_proj = grad_proj + jnp.dot(later, w_time[offset].T, preferred_element_type=jnp.float32)
     grad_proj = grad_proj.astype(jnp.bfloat16)
     grad_space, grad_time = lax.psum(
-        (
-            lax.dot_general(aggregate, grad_proj, contract, preferred_element_type=jnp.float32),
-            jnp.stack(parts),
+        lax.psum(
+            (
+                lax.dot_general(aggregate, grad_proj, contract, preferred_element_type=jnp.float32),
+                jnp.stack(parts),
+            ),
+            ("gy", "ta"),
         ),
-        ("gx", "gy", "ta"),
+        "gx",
     )
     return (updated, grad_space * row_scale, grad_time * row_scale)
 

time: 479 us -> 689 us (1.44)
  waiting for transfers between devices: 327 us -> 537 us
    psum x1, waiting for transfers between devices: 152 us -> 292 us  [shards(): lax.psum((lax.dot_general(aggregate, grad_proj, contract, preferred_eleme...]
    psum x0 -> x1, waiting for transfers between devices: none -> 69.9 us  [shards(): lax.psum(lax.psum((lax.dot_general(aggregate, grad_proj, contract, prefer...]
  transfers between devices with their start and end apart: 7 -> 8, of which waited for: 6 -> 7; matrix products, arithmetic and copies ran while one was open for 4% -> 3% of each run, Pallas kernels for 0% -> 0%
where the time goes in v1:
time: 689 us; the launch traced here: 688 us
  waiting for transfers between devices  537 us (78%)
  matrix products  67.5 us (10%)
  local copies, waits for them, and re-layouts  40.2 us (6%)
  other arithmetic  15.3 us (2%)
  between operations  14.3 us (2%)
  starting transfers between devices  13.7 us (2%)
    psum x1, waiting for transfers between devices, shards(): lax.psum((lax.dot_general(aggregate, grad_proj, contract, preferred_eleme...  292 us
    ppermute x2, waiting for transfers between devices, from_behind(): return lax.ppermute(block, axis, route)  124 us
    psum x1, waiting for transfers between devices, shards(): lax.psum(lax.psum((lax.dot_general(aggregate, grad_proj, contract, prefer...  69.9 us
    ppermute x2, waiting for transfers between devices, with_halo(): lax.ppermute(lax.slice_in_dim(block, block.shape[dim] - width, None, axis...  51.2 us
    gather x4, local copies, waits for them, and re-layouts, shards(): picked = jnp.take(flat_tiles, source_index, axis=1)  25.9 us
    dot_general x5, matrix products, shards(): jnp.dot(window, w_time[offset], preferred_element_type=jnp.float32)  24.4 us
    dot_general x4, matrix products, shards(): jnp.einsum('tij,ftjc->ftic', lipid_mask, picked, preferred_element_type=j...  23.1 us
  transfers between devices with their start and end apart: 8, of which 7 were waited for; matrix products, arithmetic and copies ran while one was open for 3% of the time, Pallas kernels for 0%

profile of v1, /device:TPU:1, one launch (start us, length us, event | category | flops | bytes accessed | tf_op | source)
XLA Modules:
  0.0 688.1 jit_solution(5378337485440147880)
XLA Ops:
  7.2 1.8 fusion.64
  9.1 4.4 collective-permute-start
  13.5 22.5 %collective-permute-done = bf16[4,1,4,128,256]{4,3,2,1,0:T(8,128)(2,1)S(1)} collective-permute-done((bf16[4,1,4,128,256]{4,3,2,1,0:T(8,128)(2,1)S(1)}, bf16[4,1,4,128,256]{4,3,2,1,0:T(8,128)(2,1)S(1)}, u32[]{:S(2)}, u32[]{:S(2)}) %collective-permute-start) | collective-permute-done | bytes 1048608 | tf_op jit(solution)/shard_map/ppermute | solution.py:14
  36.1 0.5 constant_dynamic-update-slice_fusion.1
  36.9 2.7 copy-done.4
  39.6 1.9 fusion.63
  41.5 1.7 collective-permute-start.2
  43.2 2.1 collective-permute-start.3
  45.5 0.4 fusion.54
  46.3 0.7 divide_reduce_fusion
  47.7 2.8 convert.11
  50.6 1.1 fusion.65
  51.7 28.7 %collective-permute-done.2 = bf16[4,6,1,128,256]{4,3,2,1,0:T(8,128)(2,1)S(1)} collective-permute-done((bf16[4,6,1,128,256]{4,3,2,1,0:T(8,128)(2,1)}, bf16[4,6,1,128,256]{4,3,2,1,0:T(8,128)(2,1)S(1)}, u32[]{:S(2)}, u32[]{:S(2)}) %collective-permute-start.2) | collective-permute-done | bytes 1572896 | tf_op jit(solution)/shard_map/ppermute | solution.py:14
  80.4 5.7 pad_maximum_fusion
  86.1 6.4 gather_fusion.3
  92.5 6.5 gather_fusion.2
  99.0 6.6 gather_fusion.1
  105.6 6.5 gather_fusion
  112.1 3.8 fusion.8
  115.9 4.5 fusion.12
  120.5 4.5 fusion.10
  125.0 10.2 %fusion.5 = bf16[4,16,128,256]{3,2,0,1:T(8,128)(2,1)} fusion(f32[16,4,256,128]{2,3,1,0:T(8,128)S(1)} %fusion.8, f32[16,4,256,128]{2,3,1,0:T(8,128)} %fusion.12, f32[16,4,256,128]{2,3,1,0:T(8,128)} %fusion.10, bf16[16,128,128,1]{2,1,3,0:T(8,128)(2,1)S(1)} %bitcast.119, bf16[16,4,128,256]{3,2,1,0:T(8,128)(2,1)} %gather_fusion.3, ...), kind=kOutput, calls=%fused_computation.20 | convolution fusion | flops 549453824 | bytes 34078736 | tf_op jit(solution)/shard_map/tij,ftjc->ftic/dot_general | solution.py:49
  135.2 2.5 copy.9
  137.7 1.2 convolution_convert_fusion
  138.9 0.6 copy-done.3
  139.7 0.9 copy-done.9
  140.6 0.7 fusion.29
  141.3 0.7 convolution_add_fusion.2
  142.0 4.1 collective-permute-start.4
  146.2 4.5 fusion.35
  150.6 4.5 fusion.38
  155.1 78.7 %collective-permute-done.4 = f32[2,2048,256]{2,1,0:T(8,128)} collective-permute-done((f32[2,2048,256]{2,1,0:T(8,128)S(1)}, f32[2,2048,256]{2,1,0:T(8,128)}, u32[]{:S(2)}, u32[]{:S(2)}) %collective-permute-start.4) | collective-permute-done | bytes 4194336 | tf_op jit(solution)/shard_map/ppermute | solution.py:25
  233.8 14.0 %fusion.2 = (bf16[4,2048,256]{2,1,0:T(8,128)(2,1)S(1)}, bf16[4,2048,256]{2,1,0:T(8,128)(2,1)}) fusion(bf16[4,4,4,128,256]{4,3,2,1,0:T(8,128)(2,1)} %param.13, bf16[4,4,4,128,256]{4,3,2,1,0:T(8,128)(2,1)} %param.8, f32[2,2048,256]{2,1,0:T(8,128)} %collective-permute-done.4, bf16[4,2048,256]{2,1,0:T(8,128)(2,1)S(1)} %bitcast.105, ...), kind=kOutput, calls=%fused_computation.11 | convolution fusion | flops 572522496 | bytes 42074112 | tf_op jit(solution)/shard_map/dot_general | solution.py:60
  247.9 1.3 collective-permute-start.5
  249.2 1.3 fusion.40
  250.5 1.3 convolution_bitcast_fusion.2
  251.8 45.1 %collective-permute-done.5 = bf16[2,2048,256]{2,1,0:T(8,128)(2,1)S(1)} collective-permute-done((bf16[2,2048,256]{2,1,0:T(8,128)(2,1)S(1)}, bf16[2,2048,256]{2,1,0:T(8,128)(2,1)S(1)}, u32[]{:S(2)}, u32[]{:S(2)}) %collective-permute-start.5) | collective-permute-done | bytes 2097184 | tf_op jit(solution)/shard_map/ppermute | solution.py:25
  296.9 0.8 pad_maximum_fusion.1
  297.8 1.3 convolution_bitcast_fusion.1
  299.1 0.7 copy-done.2
  299.8 1.3 convolution_bitcast_fusion
  301.1 4.5 convolution_add_fusion.1
  305.6 9.1 %fusion.28 = f32[256,256]{1,0:T(8,128)} fusion(bf16[8192,256]{1,0:T(8,128)(2,1)} %bitcast.117, f32[8192,256]{1,0:T(8,128)} %convolution_add_fusion.1, bf16[8192,256]{1,0:T(8,128)(2,1)} %bitcast.115, bf16[3,256,256]{2,1,0:T(8,128)(2,1)S(1)} %copy-done.9), kind=kOutput, calls=%fused_computation.47 | convolution fusion | flops 2151677952 | bytes 17170432 | tf_op jit(solution)/shard_map/dot_general | solution.py:101
  314.7 0.9 pad_maximum_fusion.2
  315.7 291.9 %all-reduce.8.cloned.1.call-done = (f32[256,256]{1,0:T(8,128)}, f32[3,256,256]{2,1,0:T(8,128)}) async-done(((f32[256,256]{1,0:T(8,128)}, f32[3,256,256]{2,1,0:T(8,128)}), (f32[256,256]{1,0:T(8,128)}, f32[3,256,256]{2,1,0:T(8,128)})) %all-reduce.8.cloned.1.call-update) | async-done | bytes 1048592 | tf_op jit(solution)/shard_map/psum | solution.py:99
  607.6 69.9 %all-reduce.10.cloned.1.call-done = (f32[256,256]{1,0:T(8,128)}, f32[3,256,256]{2,1,0:T(8,128)}) async-done(((f32[256,256]{1,0:T(8,128)}, f32[3,256,256]{2,1,0:T(8,128)}), (f32[256,256]{1,0:T(8,128)}, f32[3,256,256]{2,1,0:T(8,128)})) %all-reduce.10.cloned.1.call-update) | async-done | bytes 1048592 | tf_op jit(solution)/shard_map/psum | solution.py:98
  677.5 1.7 broadcast_multiply_fusion.1
  679.2 2.1 broadcast_multiply_fusion
  (50 shorter events, 2.1 us)
Async XLA Ops:
  7.2 130.5 %copy-start = (bf16[256,256]{1,0:T(8,128)(2,1)S(1)}, bf16[256,256]{1,0:T(8,128)(2,1)}, u32[]{:S(2)}) copy-start(bf16[256,256]{1,0:T(8,128)(2,1)} %param.11) | copy-start | bytes 393220
  7.2 600.4 %all-reduce.8.cloned.1.call-start = ((), (), s32[]{:S(2)}) async-start(), calls=%async_computation | async-start | bytes 2097152 | tf_op jit(solution)/shard_map/psum | solution.py:99
  7.2 28.8 %copy-start.8 = (bf16[4,4,4,128,256]{4,3,2,1,0:T(8,128)(2,1)S(1)}, bf16[4,4,4,128,256]{4,3,2,1,0:T(8,128)(2,1)}, u32[]{:S(2)}) copy-start(bf16[4,4,4,128,256]{4,3,2,1,0:T(8,128)(2,1)} %param.8) | copy-start | bytes 12582916
  9.1 26.9 %collective-permute-start = (bf16[4,1,4,128,256]{4,3,2,1,0:T(8,128)(2,1)S(1)}, bf16[4,1,4,128,256]{4,3,2,1,0:T(8,128)(2,1)S(1)}, u32[]{:S(2)}, u32[]{:S(2)}) collective-permute-start(bf16[4,1,4,128,256]{4,3,2,1,0:T(8,128)(2,1)S(1)} %get-tuple-element.35), channel_id=1, source_target_pairs={{0,32},{32,64},{64,96},{96,0},{1,33},{33,65},{65,97},{97,1},{2,34}... | collective-permute-start | bytes 3145736 | tf_op jit(solution)/shard_map/ppermute | solution.py:14
  13.5 23.4 %collective-permute-start.1 = (bf16[4,1,4,128,256]{4,3,2,1,0:T(8,128)(2,1)S(1)}, bf16[4,1,4,128,256]{4,3,2,1,0:T(8,128)(2,1)S(1)}, u32[]{:S(2)}, u32[]{:S(2)}) collective-permute-start(bf16[4,1,4,128,256]{4,3,2,1,0:T(8,128)(2,1)S(1)} %get-tuple-element.34), channel_id=1, source_target_pairs={{32,0},{64,32},{96,64},{0,96},{33,1},{65,33},{97,65},{1,97},{34,2}... | collective-permute-start | bytes 3145736 | tf_op jit(solution)/shard_map/ppermute | solution.py:17
  36.6 8.9 %copy-start.11 = (s32[4,4,4]{2,1,0:T(4,128)S(1)}, s32[4,4,4]{2,1,0:T(4,128)}, u32[]{:S(2)}) copy-start(s32[4,4,4]{2,1,0:T(4,128)} %param.9) | copy-start | bytes 772
  36.9 2.7 copy-start.4
  41.5 38.9 %collective-permute-start.2 = (bf16[4,6,1,128,256]{4,3,2,1,0:T(8,128)(2,1)}, bf16[4,6,1,128,256]{4,3,2,1,0:T(8,128)(2,1)S(1)}, u32[]{:S(2)}, u32[]{:S(2)}) collective-permute-start(bf16[4,6,1,128,256]{4,3,2,1,0:T(8,128)(2,1)} %get-tuple-element.32), channel_id=1, source_target_pairs={{0,8},{8,16},{16,24},{24,0},{1,9},{9,17},{17,25},{25,1},{2,10},{10... | collective-permute-start | bytes 4718600 | tf_op jit(solution)/shard_map/ppermute | solution.py:14
  43.2 37.2 %collective-permute-start.3 = (bf16[4,6,1,128,256]{4,3,2,1,0:T(8,128)(2,1)}, bf16[4,6,1,128,256]{4,3,2,1,0:T(8,128)(2,1)}, u32[]{:S(2)}, u32[]{:S(2)}) collective-permute-start(bf16[4,6,1,128,256]{4,3,2,1,0:T(8,128)(2,1)} %get-tuple-element.33), channel_id=1, source_target_pairs={{8,0},{16,8},{24,16},{0,24},{9,1},{17,9},{25,17},{1,25},{10,2},{18... | collective-permute-start | bytes 4718600 | tf_op jit(solution)/shard_map/ppermute | solution.py:17
  47.6 32.7 %copy-start.5 = (bf16[4,6,4,128,256]{4,3,2,1,0:T(8,128)(2,1)S(1)}, bf16[4,6,4,128,256]{4,3,2,1,0:T(8,128)(2,1)}, u32[]{:S(2)}) copy-start(bf16[4,6,4,128,256]{4,3,2,1,0:T(8,128)(2,1)} %copy-done.4) | copy-start | bytes 18874372
  112.1 3.8 copy-start.7
  112.1 3.8 copy-start.10
  115.9 4.6 copy-start.6
  137.7 1.9 copy-start.3
  139.6 1.0 copy-start.9
  142.0 91.8 %collective-permute-start.4 = (f32[2,2048,256]{2,1,0:T(8,128)S(1)}, f32[2,2048,256]{2,1,0:T(8,128)}, u32[]{:S(2)}, u32[]{:S(2)}) collective-permute-start(f32[2,2048,256]{2,1,0:T(8,128)S(1)} %convolution_add_fusion.2), channel_id=1, source_target_pairs={{0,1},{1,2},{2,3},{3,4},{4,5},{5,6},{6,7},{8,9},{9,10},{10,11},{11... | collective-permute-start | bytes 12582920 | tf_op jit(solution)/shard_map/ppermute | solution.py:25
  247.9 49.0 %collective-permute-start.5 = (bf16[2,2048,256]{2,1,0:T(8,128)(2,1)S(1)}, bf16[2,2048,256]{2,1,0:T(8,128)(2,1)S(1)}, u32[]{:S(2)}, u32[]{:S(2)}) collective-permute-start(bf16[2,2048,256]{2,1,0:T(8,128)(2,1)S(1)} %slice.118), channel_id=1, source_target_pairs={{1,0},{2,1},{3,2},{4,3},{5,4},{6,5},{7,6},{9,8},{10,9},{11,10},{12... | collective-permute-start | bytes 6291464 | tf_op jit(solution)/shard_map/ppermute | solution.py:25
  297.8 2.0 copy-start.2
  305.6 375.6 %copy-start.1 = (bf16[256,256]{1,0:T(8,128)(2,1)S(1)}, bf16[256,256]{1,0:T(8,128)(2,1)}, u32[]{:S(2)}) copy-start(bf16[256,256]{1,0:T(8,128)(2,1)} %param.11) | copy-start | bytes 393220
  315.7 361.8 %all-reduce.10.cloned.1.call-start = ((), (), s32[]{:S(2)}) async-start(), calls=%async_computation.1 | async-start | bytes 2097152 | tf_op jit(solution)/shard_map/psum | solution.py:98
Sparse Core Ops, SparseCore 0:
  315.8 291.7 all-reduce.7
  610.4 67.0 all-reduce.9
